TPU v7x, 256 devices: a whole 4x4x8 slice. The times are simulated.
256 devices in a mesh: row: 16 (over z, core), col: 16 (over y, x).
Axes of the slice: x: 4, y: 4, z: 8, core: 2. Of those that a mesh axis runs over, the one named last changes fastest.
Arguments:
- source_embed: bfloat16 [32768, 256], P('row'), may hold values from -16 to 16
- target_embed: bfloat16 [32768, 256], P('col'), may hold values from -16 to 16
- source_logmass: float32 [32768], P('row'), may hold values from -6 to 6
- target_logmass: float32 [32768], P('col'), may hold values from -6 to 6
- tile_rows: int32 [16, 16, 128], P('row', 'col'), may hold values from 0 to 15, as said below
- tile_columns: int32 [16, 16, 128], P('row', 'col'), may hold values from 0 to 15, as said below
- tile_counts: int32 [16, 16], P('row', 'col'), may hold values from 16 to 128, as said below
- row_cotangent: float32 [32768], P('row'), may hold values from -6 to 6
- column_cotangent: float32 [32768], P('col'), may hold values from -6 to 6
Outputs:
- source_potential: float32 [32768], P('row')
- target_potential: float32 [32768], P('col')
- source_grad: float32 [32768, 256], P(('row', 'col'))
- target_grad: float32 [32768, 256], P(('col', 'row'))
Inputs may be any that keep to these rules, and one draw needn't show every extreme that they name: `tile_rows`: the valid slots of one device name distinct tiles; its first 16 slots are the tiles (k, k) for k = 0 .. 15 in order; slots at or after the device's count hold 0. `tile_columns`: as tile_rows; slots at or after the device's count hold 0. `tile_counts`: some device has all 128 slots valid.
All inputs are finite; a program needn't handle non-finite values.
Results may differ from a plain program's by a relative error of at most 0.01.
Values sent between devices are 32-bit elements; how exact they have to be, the bound alone decides.
A program may use at most 128 MiB of HBM per device.

v0:
```python
import jax
import jax.numpy as jnp
from jax import lax
from jax.sharding import PartitionSpec as P

TB = 128
ITERS = 3


floor_value = -1e30
slots_per_step = 8


def row_lse(partial_max, partial_sum):
    largest = lax.pmax(partial_max, "col")
    summed = lax.psum(partial_sum * jnp.exp(partial_max - largest), "col")
    return largest + jnp.log(summed)


def col_lse(partial_max, partial_sum):
    largest = lax.pmax(partial_max, "row")
    summed = lax.psum(partial_sum * jnp.exp(partial_max - largest), "row")
    return largest + jnp.log(summed)


def on_device(
    source_embed,
    target_embed,
    source_logmass,
    target_logmass,
    tile_rows,
    tile_columns,
    tile_counts,
    row_cotangent,
    column_cotangent,
):
    cell_total, embed_width = source_embed.shape
    block_count = cell_total // TB
    row_list = tile_rows.reshape(-1)
    col_list = tile_columns.reshape(-1)
    slot_total = row_list.shape[0]
    live_count = tile_counts.reshape(-1)[0]
    steps_live = (live_count + slots_per_step - 1) // slots_per_step
    source_blocks = source_embed.reshape(block_count, TB, embed_width)
    target_blocks = target_embed.reshape(block_count, TB, embed_width)

    def fetch(slot_step):
        first_slot = slot_step * slots_per_step
        row_ids = lax.dynamic_slice_in_dim(row_list, first_slot, slots_per_step)
        col_ids = lax.dynamic_slice_in_dim(col_list, first_slot, slots_per_step)
        live_slot = first_slot + jnp.arange(slots_per_step, dtype=jnp.int32) < live_count
        return (first_slot, row_ids, col_ids, live_slot)

    def compute_scores(row_ids, col_ids):
        return jnp.einsum(
            "gpe,gqe->gpq",
            source_blocks[row_ids],
            target_blocks[col_ids],
            preferred_element_type=jnp.float32,
        )

    def fill_scores(slot_step, score_table):
        first_slot, row_ids, col_ids, live_slot = fetch(slot_step)
        return lax.dynamic_update_slice_in_dim(
            score_table, compute_scores(row_ids, col_ids), first_slot, 0
        )

    score_table = lax.fori_loop(
        0, steps_live, fill_scores, jnp.zeros((slot_total, TB, TB), jnp.float32)
    )

    def scores_at(first_slot):
        return lax.dynamic_slice_in_dim(score_table, first_slot, slots_per_step, 0)

    def lse_partial(vector, by_rows):
        vector_blocks = vector.reshape(block_count, TB)

        def lse_advance(slot_step, state):
            old_max, old_sum = state
            first_slot, row_ids, col_ids, live_slot = fetch(slot_step)
            scores = scores_at(first_slot)
            if by_rows:
                own_ids = row_ids
                shifted = scores + vector_blocks[col_ids][:, None, :]
            else:
                own_ids = col_ids
                shifted = jnp.swapaxes(scores, 1, 2) + vector_blocks[row_ids][:, None, :]
            tile_max = jnp.where(live_slot[:, None], jnp.max(shifted, axis=2), floor_value)
            new_max = old_max.at[own_ids].max(tile_max)
            terms = jnp.sum(jnp.exp(shifted - new_max[own_ids][:, :, None]), axis=2)
            terms = jnp.where(live_slot[:, None], terms, 0.0)
            rescaled = old_sum * jnp.exp(old_max - new_max)
            return (new_max, rescaled.at[own_ids].add(terms))

        start_state = (
            jnp.full((block_count, TB), floor_value, jnp.float32),
            jnp.zeros((block_count, TB), jnp.float32),
        )
        final_max, final_sum = lax.fori_loop(0, steps_live, lse_advance, start_state)
        return (final_max.reshape(-1), final_sum.reshape(-1))

    col_pot = jnp.zeros((cell_total,), jnp.float32)
    row_pots = []
    col_pots = [col_pot]
    for iteration in range(ITERS):
        row_pot = source_logmass - row_lse(*lse_partial(col_pot, True))
        col_pot = target_logmass - col_lse(*lse_partial(row_pot, False))
        row_pots.append(row_pot)
        col_pots.append(col_pot)

    def adjoint_pass(row_add, col_add, weights, by_rows, accum_tiles):
        row_blocks = row_add.reshape(block_count, TB)
        col_blocks = col_add.reshape(block_count, TB)
        weight_blocks = weights.reshape(block_count, TB)

        def adjoint_advance(slot_step, state):
            totals, accum = state
            first_slot, row_ids, col_ids, live_slot = fetch(slot_step)
            scores = scores_at(first_slot)
            plan = jnp.exp(
                scores + row_blocks[row_ids][:, :, None] + col_blocks[col_ids][:, None, :]
            )
            plan = jnp.where(live_slot[:, None, None], plan, 0.0)
            if by_rows:
                weighted = plan * weight_blocks[col_ids][:, None, :]
                partial_value = jnp.sum(weighted, axis=2)
                own_ids = row_ids
            else:
                weighted = plan * weight_blocks[row_ids][:, :, None]
                partial_value = jnp.sum(weighted, axis=1)
                own_ids = col_ids
            totals = totals.at[own_ids].add(partial_value)
            previous = lax.dynamic_slice_in_dim(accum, first_slot, slots_per_step, 0)
            accum = lax.dynamic_update_slice_in_dim(accum, previous - weighted, first_slot, 0)
            return (totals, accum)

        start_state = (jnp.zeros((block_count, TB), jnp.float32), accum_tiles)
        totals, accum_tiles = lax.fori_loop(0, steps_live, adjoint_advance, start_state)
        return (totals.reshape(-1), accum_tiles)

    accum_tiles = jnp.zeros((slot_total, TB, TB), jnp.float32)
    col_adj = column_cotangent
    for iteration in reversed(range(ITERS)):
        partial_value, accum_tiles = adjoint_pass(
            row_pots[iteration],
            col_pots[iteration + 1] - target_logmass,
            col_adj,
            True,
            accum_tiles,
        )
        summed = lax.psum(partial_value, "col")
        if iteration == ITERS - 1:
            row_adj = row_cotangent - summed
        else:
            row_adj = -summed
        partial_value, accum_tiles = adjoint_pass(
            row_pots[iteration] - source_logmass, col_pots[iteration], row_adj, False, accum_tiles
        )
        if iteration > 0:
            col_adj = -lax.psum(partial_value, "row")

    def grad_step(slot_step, state):
        grad_src, grad_tgt = state
        first_slot, row_ids, col_ids, live_slot = fetch(slot_step)
        rounded = lax.dynamic_slice_in_dim(accum_tiles, first_slot, slots_per_step, 0).astype(
            jnp.bfloat16
        )
        row_terms = jnp.einsum(
            "gpq,gqe->gpe", rounded, target_blocks[col_ids], preferred_element_type=jnp.float32
        )
        col_terms = jnp.einsum(
            "gpq,gpe->gqe", rounded, source_blocks[row_ids], preferred_element_type=jnp.float32
        )
        row_terms = jnp.where(live_slot[:, None, None], row_terms, 0.0)
        col_terms = jnp.where(live_slot[:, None, None], col_terms, 0.0)
        return (grad_src.at[row_ids].add(row_terms), grad_tgt.at[col_ids].add(col_terms))

    zero_grads = jnp.zeros((block_count, TB, embed_width), jnp.float32)
    grad_src, grad_tgt = lax.fori_loop(0, steps_live, grad_step, (zero_grads, zero_grads))
    grad_src = grad_src.reshape(cell_total, embed_width)
    grad_tgt = grad_tgt.reshape(cell_total, embed_width)
    source_grad = lax.psum_scatter(grad_src, "col", scatter_dimension=0, tiled=True)
    target_grad = lax.psum_scatter(grad_tgt, "row", scatter_dimension=0, tiled=True)
    return (row_pots[-1], col_pots[-1], source_grad, target_grad)


def solution(mesh):
    placed = (
        P("row", None),
        P("col", None),
        P("row"),
        P("col"),
        P("row", "col", None),
        P("row", "col", None),
        P("row", "col"),
        P("row"),
        P("col"),
    )
    return jax.shard_map(
        on_device,
        mesh=mesh,
        in_specs=placed,
        out_specs=(P("row"), P("col"), P(("row", "col"), None), P(("col", "row"), None)),
        check_vma=False,
    )
```

profile of v0, /device:TPU:1, one launch (start us, length us, event | category | flops | bytes accessed | tf_op | source)
XLA Modules:
  0.0 2019.7 jit_solution(17156398659517074911)
XLA Ops:
  8.0 4.3 broadcast.242.clone
  12.3 14.5 while.166
  26.8 24.0 %while.167 = (s32[]{:T(128)}, f32[16,128]{1,0:T(8,128)S(1)}, f32[16,128]{1,0:T(8,128)S(1)}, s32[]{:T(128)}, s32[128]{0:T(128)S(1)}, /*index=5*/s32[]{:T(128)}, f...) while((s32[]{:T(128)}, f32[16,128]{1,0:T(8,128)S(1)}, ...), condition=%wide.region_7.8_spmd, body=%wide.region_2.7_spmd.sunk | while | flops 663622 | bytes 1193435 | solution.py:99
  50.8 146.3 %pmax.42 = f32[2048]{0:T(1024)S(1)} all-reduce(f32[2048]{0:T(1024)S(1)} %bitcast.128), channel_id=1, replica_groups=mesh['row'=16,'col'=16] {'col'}, use_global_device_ids=true, to_apply=%region_8.9 | all-reduce | flops 2048 | bytes 16384 | tf_op jit(solution)/shard_map/pmax | solution.py:15
  197.1 29.0 %psum.77 = f32[2048]{0:T(1024)S(1)} all-reduce(f32[2048]{0:T(1024)S(1)} %bitcast_multiply_fusion.5), channel_id=1, replica_groups=mesh['row'=16,'col'=16] {'col'}, use_global_device_ids=true, to_apply=%region_9.10 | all-reduce | flops 2048 | bytes 16384 | tf_op jit(solution)/shard_map/psum | solution.py:16
  226.2 23.4 %while.168 = (s32[]{:T(128)}, f32[16,128]{1,0:T(8,128)S(1)}, f32[16,128]{1,0:T(8,128)S(1)}, s32[]{:T(128)}, s32[128]{0:T(128)S(1)}, /*index=5*/s32[]{:T(128)}, f...) while((s32[]{:T(128)}, f32[16,128]{1,0:T(8,128)S(1)}, ...), condition=%wide.region_15.16_spmd, body=%wide.region_10.15_spmd.sunk | while | flops 663622 | bytes 1185247 | solution.py:99
  249.6 107.3 %pmax.43 = f32[2048]{0:T(1024)S(1)} all-reduce(f32[2048]{0:T(1024)S(1)} %bitcast.129), channel_id=1, replica_groups=mesh['row'=16,'col'=16] {'row'}, use_global_device_ids=true, to_apply=%region_16.17 | all-reduce | flops 2048 | bytes 16384 | tf_op jit(solution)/shard_map/pmax | solution.py:21
  356.9 23.5 %psum.78 = f32[2048]{0:T(1024)S(1)} all-reduce(f32[2048]{0:T(1024)S(1)} %bitcast_multiply_fusion.4), channel_id=1, replica_groups=mesh['row'=16,'col'=16] {'row'}, use_global_device_ids=true, to_apply=%region_17.18 | all-reduce | flops 2048 | bytes 16384 | tf_op jit(solution)/shard_map/psum | solution.py:22
  380.5 24.0 %while.169 = (s32[]{:T(128)}, f32[16,128]{1,0:T(8,128)S(1)}, f32[16,128]{1,0:T(8,128)S(1)}, s32[]{:T(128)}, s32[128]{0:T(128)S(1)}, /*index=5*/s32[]{:T(128)}, f...) while((s32[]{:T(128)}, f32[16,128]{1,0:T(8,128)S(1)}, ...), condition=%wide.region_23.24_spmd, body=%wide.region_18.23_spmd.sunk | while | flops 663622 | bytes 1185247 | solution.py:99
  404.5 100.7 %pmax.44 = f32[2048]{0:T(1024)S(1)} all-reduce(f32[2048]{0:T(1024)S(1)} %bitcast.130), channel_id=1, replica_groups=mesh['row'=16,'col'=16] {'col'}, use_global_device_ids=true, to_apply=%region_24.25 | all-reduce | flops 2048 | bytes 16384 | tf_op jit(solution)/shard_map/pmax | solution.py:15
  505.2 29.1 %psum.79 = f32[2048]{0:T(1024)S(1)} all-reduce(f32[2048]{0:T(1024)S(1)} %bitcast_multiply_fusion.3), channel_id=1, replica_groups=mesh['row'=16,'col'=16] {'col'}, use_global_device_ids=true, to_apply=%region_25.26 | all-reduce | flops 2048 | bytes 16384 | tf_op jit(solution)/shard_map/psum | solution.py:16
  534.4 23.4 %while.170 = (s32[]{:T(128)}, f32[16,128]{1,0:T(8,128)S(1)}, f32[16,128]{1,0:T(8,128)S(1)}, s32[]{:T(128)}, s32[128]{0:T(128)S(1)}, /*index=5*/s32[]{:T(128)}, f...) while((s32[]{:T(128)}, f32[16,128]{1,0:T(8,128)S(1)}, ...), condition=%wide.region_31.32_spmd, body=%wide.region_26.31_spmd.sunk | while | flops 663622 | bytes 1185247 | solution.py:99
  557.8 106.0 %pmax.45 = f32[2048]{0:T(1024)S(1)} all-reduce(f32[2048]{0:T(1024)S(1)} %bitcast.131), channel_id=1, replica_groups=mesh['row'=16,'col'=16] {'row'}, use_global_device_ids=true, to_apply=%region_32.33 | all-reduce | flops 2048 | bytes 16384 | tf_op jit(solution)/shard_map/pmax | solution.py:21
  663.8 23.5 %psum.80 = f32[2048]{0:T(1024)S(1)} all-reduce(f32[2048]{0:T(1024)S(1)} %bitcast_multiply_fusion.2), channel_id=1, replica_groups=mesh['row'=16,'col'=16] {'row'}, use_global_device_ids=true, to_apply=%region_33.34 | all-reduce | flops 2048 | bytes 16384 | tf_op jit(solution)/shard_map/psum | solution.py:22
  687.4 24.0 %while.171 = (s32[]{:T(128)}, f32[16,128]{1,0:T(8,128)S(1)}, f32[16,128]{1,0:T(8,128)S(1)}, s32[]{:T(128)}, s32[128]{0:T(128)S(1)}, /*index=5*/s32[]{:T(128)}, f...) while((s32[]{:T(128)}, f32[16,128]{1,0:T(8,128)S(1)}, ...), condition=%wide.region_39.40_spmd, body=%wide.region_34.39_spmd.sunk | while | flops 663622 | bytes 1185247 | solution.py:99
  711.5 94.5 %pmax.46 = f32[2048]{0:T(1024)S(1)} all-reduce(f32[2048]{0:T(1024)S(1)} %bitcast.132), channel_id=1, replica_groups=mesh['row'=16,'col'=16] {'col'}, use_global_device_ids=true, to_apply=%region_40.41 | all-reduce | flops 2048 | bytes 16384 | tf_op jit(solution)/shard_map/pmax | solution.py:15
  806.0 29.1 %psum.81 = f32[2048]{0:T(1024)S(1)} all-reduce(f32[2048]{0:T(1024)S(1)} %bitcast_multiply_fusion.1), channel_id=1, replica_groups=mesh['row'=16,'col'=16] {'col'}, use_global_device_ids=true, to_apply=%region_41.42 | all-reduce | flops 2048 | bytes 16384 | tf_op jit(solution)/shard_map/psum | solution.py:16
  835.1 23.4 %while.172 = (s32[]{:T(128)}, f32[16,128]{1,0:T(8,128)S(1)}, f32[16,128]{1,0:T(8,128)S(1)}, s32[]{:T(128)}, s32[128]{0:T(128)S(1)}, /*index=5*/s32[]{:T(128)}, f...) while((s32[]{:T(128)}, f32[16,128]{1,0:T(8,128)S(1)}, ...), condition=%wide.region_47.48_spmd, body=%wide.region_42.47_spmd.sunk | while | flops 663622 | bytes 1185247 | solution.py:99
  858.5 112.3 %pmax.47 = f32[2048]{0:T(1024)S(1)} all-reduce(f32[2048]{0:T(1024)S(1)} %bitcast.133), channel_id=1, replica_groups=mesh['row'=16,'col'=16] {'row'}, use_global_device_ids=true, to_apply=%region_48.49 | all-reduce | flops 2048 | bytes 16384 | tf_op jit(solution)/shard_map/pmax | solution.py:21
  970.8 23.5 %psum.82 = f32[2048]{0:T(1024)S(1)} all-reduce(f32[2048]{0:T(1024)S(1)} %bitcast_multiply_fusion), channel_id=1, replica_groups=mesh['row'=16,'col'=16] {'row'}, use_global_device_ids=true, to_apply=%region_49.50 | all-reduce | flops 2048 | bytes 16384 | tf_op jit(solution)/shard_map/psum | solution.py:22
  994.9 4.3 broadcast.242
  999.2 21.3 %while.173 = (s32[]{:T(128)}, f32[16,128]{1,0:T(8,128)S(1)}, f32[128,128,128]{2,1,0:T(8,128)}, s32[]{:T(128)}, s32[128]{0:T(128)S(1)}, /*index=5*/s32[]{:T(128)}...) while((s32[]{:T(128)}, f32[16,128]{1,0:T(8,128)S(1)}, ...), condition=%wide.region_53.54_spmd, body=%wide.region_50.53_spmd.sunk | while | flops 788550 | bytes 1634843 | solution.py:138
  1020.5 80.5 %psum.83 = f32[2048]{0:T(1024)S(1)} all-reduce(f32[2048]{0:T(1024)S(1)} %bitcast.120), channel_id=1, replica_groups=mesh['row'=16,'col'=16] {'col'}, use_global_device_ids=true, to_apply=%region_54.55 | all-reduce | flops 2048 | bytes 16384 | tf_op jit(solution)/shard_map/psum | solution.py:151
  1101.0 21.8 %while.174 = (s32[]{:T(128)}, f32[16,128]{1,0:T(8,128)S(1)}, f32[128,128,128]{2,1,0:T(8,128)}, s32[]{:T(128)}, s32[128]{0:T(128)S(1)}, /*index=5*/s32[]{:T(128)}...) while((s32[]{:T(128)}, f32[16,128]{1,0:T(8,128)S(1)}, ...), condition=%wide.region_58.59_spmd, body=%wide.region_55.58_spmd.sunk | while | flops 788550 | bytes 1634843 | solution.py:138
  1103.5 2.4 subtract_dynamic-update-slice_fusion.13
  1109.0 2.4 subtract_dynamic-update-slice_fusion.13
  1122.9 104.3 %psum.84 = f32[2048]{0:T(1024)S(1)} all-reduce(f32[2048]{0:T(1024)S(1)} %bitcast.121), channel_id=1, replica_groups=mesh['row'=16,'col'=16] {'row'}, use_global_device_ids=true, to_apply=%region_59.60 | all-reduce | flops 2048 | bytes 16384 | tf_op jit(solution)/shard_map/psum | solution.py:160
  1227.3 21.4 %while.175 = (s32[]{:T(128)}, f32[16,128]{1,0:T(8,128)S(1)}, f32[128,128,128]{2,1,0:T(8,128)}, s32[]{:T(128)}, s32[128]{0:T(128)S(1)}, /*index=5*/s32[]{:T(128)}...) while((s32[]{:T(128)}, f32[16,128]{1,0:T(8,128)S(1)}, ...), condition=%wide.region_63.64_spmd, body=%wide.region_60.63_spmd.sunk | while | flops 788550 | bytes 1634843 | solution.py:138
  1248.6 76.2 %psum.85 = f32[2048]{0:T(1024)S(1)} all-reduce(f32[2048]{0:T(1024)S(1)} %bitcast.122), channel_id=1, replica_groups=mesh['row'=16,'col'=16] {'col'}, use_global_device_ids=true, to_apply=%region_64.65 | all-reduce | flops 2048 | bytes 16384 | tf_op jit(solution)/shard_map/psum | solution.py:151
  1324.9 21.9 %while.176 = (s32[]{:T(128)}, f32[16,128]{1,0:T(8,128)S(1)}, f32[128,128,128]{2,1,0:T(8,128)}, s32[]{:T(128)}, s32[128]{0:T(128)S(1)}, /*index=5*/s32[]{:T(128)}...) while((s32[]{:T(128)}, f32[16,128]{1,0:T(8,128)S(1)}, ...), condition=%wide.region_68.69_spmd, body=%wide.region_65.68_spmd.sunk | while | flops 788550 | bytes 1634843 | solution.py:138
  1332.8 2.4 subtract_dynamic-update-slice_fusion.15
  1346.7 108.5 %psum.86 = f32[2048]{0:T(1024)S(1)} all-reduce(f32[2048]{0:T(1024)S(1)} %bitcast.123), channel_id=1, replica_groups=mesh['row'=16,'col'=16] {'row'}, use_global_device_ids=true, to_apply=%region_69.70 | all-reduce | flops 2048 | bytes 16384 | tf_op jit(solution)/shard_map/psum | solution.py:160
  1455.3 21.4 %while.177 = (s32[]{:T(128)}, f32[16,128]{1,0:T(8,128)S(1)}, f32[128,128,128]{2,1,0:T(8,128)}, s32[]{:T(128)}, s32[128]{0:T(128)S(1)}, /*index=5*/s32[]{:T(128)}...) while((s32[]{:T(128)}, f32[16,128]{1,0:T(8,128)S(1)}, ...), condition=%wide.region_73.74_spmd, body=%wide.region_70.73_spmd.sunk | while | flops 788550 | bytes 1634843 | solution.py:138
  1476.7 82.6 %psum.87 = f32[2048]{0:T(1024)S(1)} all-reduce(f32[2048]{0:T(1024)S(1)} %bitcast.124), channel_id=1, replica_groups=mesh['row'=16,'col'=16] {'col'}, use_global_device_ids=true, to_apply=%region_74.75 | all-reduce | flops 2048 | bytes 16384 | tf_op jit(solution)/shard_map/psum | solution.py:151
  1559.3 19.5 while.178
  1566.8 2.4 subtract_dynamic-update-slice_fusion.17
  1578.8 6.3 convert.94
  1588.2 49.3 %while.179 = (s32[]{:T(128)}, f32[16,128,256]{2,1,0:T(8,128)}, f32[16,128,256]{2,1,0:T(8,128)}, s32[]{:T(128)}, s32[128]{0:T(128)S(1)}, /*index=5*/s32[]{:T(128)...) while((s32[]{:T(128)}, f32[16,128,256]{2,1,0:T(8,128)}, ...), condition=%wide.region_80.81_spmd, body=%wide.region_77.80_spmd.sunk | while | flops 135268416 | bytes 12067359 | solution.py:179
  1590.9 3.4 scatter_fusion.6
  1597.3 3.3 scatter_fusion.5
  1603.3 3.3 scatter_fusion.6
  1609.7 3.4 scatter_fusion.5
  1615.7 3.2 scatter_fusion.6
  1622.0 3.3 scatter_fusion.5
  1628.0 3.3 scatter_fusion.6
  1634.3 3.2 scatter_fusion.5
  1638.3 313.9 %reduce-scatter.3.cloned.1.call-done = f32[128,256]{1,0:T(8,128)} async-done(((f32[2048,256]{1,0:T(8,128)}), f32[128,256]{1,0:T(8,128)}) %reduce-scatter.3.cloned.1.call-update) | async-done | bytes 131088 | tf_op jit(solution)/shard_map/reduce_scatter | solution.py:182
  1952.2 60.6 %reduce-scatter.5.cloned.1.call-done = f32[128,256]{1,0:T(8,128)} async-done(((f32[2048,256]{1,0:T(8,128)}), f32[128,256]{1,0:T(8,128)}) %reduce-scatter.5.cloned.1.call-update) | async-done | bytes 131088 | tf_op jit(solution)/shard_map/reduce_scatter | solution.py:183
  (640 shorter events, 297.7 us)
Async XLA Ops:
  7.2 5.1 copy-start.3
  7.2 5.1 copy-start.4
  7.2 5.1 copy-start
  7.2 1945.0 %reduce-scatter.3.cloned.1.call-start = ((), (), s32[]{:S(2)}) async-start(), calls=%async_computation.2 | async-start | bytes 2228224 | tf_op jit(solution)/shard_map/reduce_scatter | solution.py:182
  12.3 213.9 %copy-start.5 = (f32[2048]{0:T(1024)S(1)}, f32[2048]{0:T(1024)}, u32[]{:S(2)}) copy-start(f32[2048]{0:T(1024)} %param.39) | copy-start | bytes 24580
  26.8 353.7 %copy-start.6 = (f32[2048]{0:T(1024)S(1)}, f32[2048]{0:T(1024)}, u32[]{:S(2)}) copy-start(f32[2048]{0:T(1024)} %param.40) | copy-start | bytes 24580
  711.4 287.7 %copy-start.2 = (f32[2048]{0:T(1024)S(1)}, f32[2048]{0:T(1024)}, u32[]{:S(2)}) copy-start(f32[2048]{0:T(1024)} %param.45) | copy-start | bytes 24580
  994.9 106.1 %copy-start.7 = (f32[2048]{0:T(1024)S(1)}, f32[2048]{0:T(1024)}, u32[]{:S(2)}) copy-start(f32[2048]{0:T(1024)} %param.44) | copy-start | bytes 24580
  1020.5 206.7 %copy-start.1 = (f32[16,128]{1,0:T(8,128)}, f32[16,128]{1,0:T(8,128)S(1)}, u32[]{:S(2)}) copy-start(f32[16,128]{1,0:T(8,128)S(1)} %get-tuple-element.2635) | copy-start | bytes 24580
  1637.5 375.3 %reduce-scatter.5.cloned.1.call-start = ((), (), s32[]{:S(2)}) async-start(), calls=%async_computation.3 | async-start | bytes 2228224 | tf_op jit(solution)/shard_map/reduce_scatter | solution.py:183
Sparse Core Ops, SparseCore 0:
  1637.7 314.5 reduce-scatter.2
  1955.5 57.3 reduce-scatter.4
where the time goes:
time: 2040 us; the launch traced here: 2020 us
  blocking collectives  1280 us (63%)
  waiting for transfers between devices  375 us (18%)
  other arithmetic  236 us (12%)
  local copies, waits for them, and re-layouts  97.6 us (5%)
    pmax x3, blocking collectives, row_lse(): largest = lax.pmax(partial_max, 'col')  341 us
    pmax x3, blocking collectives, col_lse(): largest = lax.pmax(partial_max, 'row')  326 us
    reduce_scatter x1, waiting for transfers between devices, on_device(): lax.psum_scatter(grad_src, 'col', scatter_dimension=0, tiled=True)  314 us
    psum x3, blocking collectives, on_device(): summed = lax.psum(partial_value, 'col')  239 us
    psum x2, blocking collectives, on_device(): col_adj = -lax.psum(partial_value, 'row')  213 us
    psum x3, blocking collectives, row_lse(): summed = lax.psum(partial_sum * jnp.exp(partial_max - largest), 'col')  87.2 us
    psum x3, blocking collectives, col_lse(): summed = lax.psum(partial_sum * jnp.exp(partial_max - largest), 'row')  70.6 us
    reduce_scatter x1, waiting for transfers between devices, on_device(): lax.psum_scatter(grad_tgt, 'row', scatter_dimension=0, tiled=True)  60.6 us
  transfers between devices with their start and end apart: 2, of which 2 were waited for; matrix products, arithmetic and copies ran while one was open for 0% of the time, Pallas kernels for 0%

commit v1 on v0

v1 whole, which is shorter than its diff:
```python
import jax
import jax.numpy as jnp
from jax import lax
from jax.experimental import pallas as pl
from jax.experimental.pallas import tpu as pltpu
from jax.sharding import PartitionSpec as P

MESH = pl.DeviceIdType.MESH
TB = 128
NB = 16
CELLS = NB * TB
E = 256
ROUNDS = 11
MASKED = -1e30
F32 = jnp.float32
BF16 = jnp.bfloat16
SHRINK = 2.0**-40
GROW = 2.0**40


def nt_dot(x, y):
    return lax.dot_general(x, y, (((1,), (1,)), ((), ())), preferred_element_type=F32)


def tn_dot(x, y):
    return lax.dot_general(x, y, (((0,), (0,)), ((), ())), preferred_element_type=F32)


def block(index, size=TB):
    return pl.ds(pl.multiple_of(index * size, size), size)


def kernel(
    src, tgt, a_ref, b_ref, rows_ref, cols_ref, count_ref, rc_ref, cc_ref,
    f_out, g_out, gs_out, gt_out,
    q, w, part, land, wide, wide2, bias, vec, vec_w, srct, xs, ys, xb, yb,
    gs_send, gs_land, gt_part, gt_sib, gt_send, gt_land,
    ar_send, ar_recv, gs_ssem, gs_rsem, sib_ssem, sib_rsem, gt_ssem, gt_rsem,
):
    row_me = lax.axis_index("row")
    col_me = lax.axis_index("col")
    z_me = row_me // 2
    core = row_me % 2
    y_me = col_me // 4
    x_me = col_me % 4

    barrier = pltpu.get_barrier_semaphore()

    @pl.loop(1, NB)
    def _(k):
        pl.semaphore_signal(
            barrier, inc=1, device_id={"row": lax.rem(row_me + k, NB)}, device_id_type=MESH
        )
        pl.semaphore_signal(
            barrier, inc=1, device_id={"col": lax.rem(col_me + k, NB)}, device_id_type=MESH
        )

    eye = lax.broadcasted_iota(jnp.int32, (TB, TB), 0) == lax.broadcasted_iota(
        jnp.int32, (TB, TB), 1
    )

    def to_row(column):
        return jnp.sum(jnp.where(eye, column, 0.0), axis=0, keepdims=True)

    def to_column(row):
        return jnp.sum(jnp.where(eye, row, 0.0), axis=1, keepdims=True)

    def widen(value):
        vec[...] = value
        for rb in range(NB):
            wide[rb * TB : (rb + 1) * TB, :] = jnp.broadcast_to(
                to_column(vec[rb : rb + 1, :]), (TB, TB)
            )

    slot = lax.broadcasted_iota(jnp.int32, (TB, TB), 1)
    which = lax.broadcasted_iota(jnp.int32, (TB, TB), 0)
    live = slot < count_ref[0, 0]
    row_hot = jnp.where((rows_ref[...] == which) & live, 1.0, 0.0).astype(BF16)
    col_hot = jnp.where((cols_ref[...] == which) & live, 1.0, 0.0).astype(BF16)
    present = nt_dot(row_hot[:NB], col_hot).astype(BF16)
    for cb in range(NB):
        spread = jnp.where(which == cb, 1.0, 0.0).astype(BF16)
        hits = jnp.dot(present, spread, preferred_element_type=F32)
        bias[:, cb * TB : (cb + 1) * TB] = jnp.where(hits > 0.5, 0.0, MASKED)

    @pl.loop(0, NB // 2)
    def _(rb):
        top = None
        left = src[block(rb, 2 * TB), :]
        for cb in range(NB // 2):
            at = slice(cb * 2 * TB, (cb + 1) * 2 * TB)
            s = nt_dot(left, tgt[at, :])
            for half in range(2):
                line = bias[pl.ds(rb * 2 + half, 1), at]
                q[block(rb * 2 + half), at] = s[half * TB : (half + 1) * TB] + line
        for half in range(2):
            here = block(rb * 2 + half)
            top = q[here, 0:TB]
            for cb in range(1, NB):
                top = jnp.maximum(top, q[here, cb * TB : (cb + 1) * TB])
            total = jnp.exp(q[here, 0:TB] - top)
            for cb in range(1, NB):
                total += jnp.exp(q[here, cb * TB : (cb + 1) * TB] - top)
            wide[here, :] = top
            wide2[here, :] = total

    for rb in range(NB):
        here = slice(rb * TB, (rb + 1) * TB)
        top = wide[here, :]
        largest = jnp.max(top, axis=1, keepdims=True)
        total = jnp.sum(wide2[here, :] * jnp.exp(top - largest), axis=1, keepdims=True)
        part[0, rb : rb + 1, :] = to_row(largest + jnp.log(total))

    pl.semaphore_wait(barrier, 2 * (NB - 1))

    def start_reduce(index, axis):
        me = row_me if axis == "row" else col_me

        @pl.loop(0, NB - 1)
        def _(k):
            if axis == "row":
                j = k // 2
                far = lax.rem(4 + (1 - 2 * (j % 2)) * ((j + 1) // 2), 8)
                peer = lax.rem(z_me + far, 8) * 2 + lax.rem(core + 1 + k, 2)
            else:
                j = k // 4
                dy = lax.rem(2 + (1 - 2 * (j % 2)) * ((j + 1) // 2), 4)
                i = k % 4
                dx = lax.rem(2 + (1 - 2 * (i % 2)) * ((i + 1) // 2), 4)
                peer = lax.rem(y_me + dy, 4) * 4 + lax.rem(x_me + dx, 4)
            pltpu.make_async_remote_copy(
                src_ref=part.at[index],
                dst_ref=land.at[index, me],
                send_sem=ar_send.at[index],
                recv_sem=ar_recv.at[index],
                device_id={axis: peer},
                device_id_type=MESH,
            ).start()

        land[index, me] = part[index]

    def end_reduce(index):
        others = land.at[index, pl.ds(0, NB - 1)]
        pltpu.make_async_copy(others, others, ar_recv.at[index]).wait()

    def summed(index):
        end_reduce(index)
        terms = [land[index, k] for k in range(NB)]
        while len(terms) > 1:
            terms = [terms[k] + terms[k + 1] for k in range(0, len(terms), 2)]
        return terms[0]

    def log_summed(index):
        end_reduce(index)
        largest = land[index, 0]
        for k in range(1, NB):
            largest = jnp.maximum(largest, land[index, k])
        total = jnp.exp(land[index, 0] - largest)
        for k in range(1, NB):
            total += jnp.exp(land[index, k] - largest)
        return largest + jnp.log(total)

    def row_pass(weights, index):
        vec_w[...] = weights

        @pl.loop(0, NB)
        def _(rb):
            here = block(rb)
            total = q[here, 0:TB] * vec_w[0:1, :]
            for cb in range(1, NB):
                total += q[here, cb * TB : (cb + 1) * TB] * vec_w[cb : cb + 1, :]
            wide[here, :] = total

        for rb in range(NB):
            total = jnp.sum(wide[rb * TB : (rb + 1) * TB, :], axis=1, keepdims=True)
            part[index, rb : rb + 1, :] = to_row(total)
        start_reduce(index, "col")

    def fold(value):
        total = value[0:8]
        for k in range(1, NB):
            total += value[k * 8 : (k + 1) * 8]
        return total

    def col_pass(weights, scale, index):
        widen(weights)

        def body(rb, totals):
            here = block(rb)
            u = wide[here, :]
            return tuple(
                totals[cb] + fold(q[here, cb * TB : (cb + 1) * TB] * u) for cb in range(NB)
            )

        totals = lax.fori_loop(0, NB, body, (jnp.zeros((8, TB), F32),) * NB)
        for cb in range(NB):
            vec[cb : cb + 1, :] = jnp.sum(totals[cb], axis=0, keepdims=True)
        part[index] = vec[...] * scale
        start_reduce(index, "row")

    start_reduce(0, "col")
    unit = jnp.where(
        lax.broadcasted_iota(jnp.int32, (E, E), 0) == lax.broadcasted_iota(jnp.int32, (E, E), 1),
        1.0,
        0.0,
    ).astype(BF16)
    for cb in range(NB // 2):
        at = slice(cb * 2 * TB, (cb + 1) * 2 * TB)
        srct[:, at] = nt_dot(unit, src[at, :]).astype(BF16)
    a = a_ref[...]
    b = b_ref[...]
    f1 = a - log_summed(0)

    widen(f1)

    def top_body(rb, tops):
        here = block(rb)
        u = wide[here, :]
        out = []
        for cb in range(NB):
            moved = q[here, cb * TB : (cb + 1) * TB] + u
            top = tops[cb]
            for k in range(NB):
                top = jnp.maximum(top, moved[k * 8 : (k + 1) * 8])
            out.append(top)
        return tuple(out)

    tops = lax.fori_loop(0, NB, top_body, (jnp.full((8, TB), MASKED, F32),) * NB)
    for cb in range(NB):
        vec_w[cb : cb + 1, :] = jnp.max(tops[cb], axis=0, keepdims=True)
    c = vec_w[...]

    def exp_body(rb, totals):
        here = block(rb)
        u = wide[here, :]
        out = []
        for cb in range(NB):
            at = slice(cb * TB, (cb + 1) * TB)
            value = jnp.exp((q[here, at] + u) - vec_w[cb : cb + 1, :])
            q[here, at] = value
            out.append(totals[cb] + fold(value))
        return tuple(out)

    totals = lax.fori_loop(0, NB, exp_body, (jnp.zeros((8, TB), F32),) * NB)
    for cb in range(NB):
        vec[cb : cb + 1, :] = jnp.sum(totals[cb], axis=0, keepdims=True)
    part[1] = c + jnp.log(vec[...])
    start_reduce(1, "row")
    exp_a = jnp.exp(a)
    exp_b = jnp.exp(b)
    inv_a = jnp.exp(-a)
    inv_b = jnp.exp(-b)
    g1 = b - log_summed(1)

    d = jnp.exp(c + g1)

    def put(ref, term, value):
        vec[...] = value
        for k in range(NB):
            ref[k * 8 + term : k * 8 + term + 1, :] = vec[k : k + 1, :]

    xs[...] = jnp.zeros_like(xs)
    ys[...] = jnp.zeros_like(ys)

    row_pass(d, 2)
    put(ys, 4, d * -SHRINK)
    put(ys, 5, jnp.exp(c) * -SHRINK)
    put(xs, 2, jnp.ones_like(a))
    u2 = exp_a / summed(2)
    col_pass(u2, d, 3)
    put(xs, 1, u2)
    v2 = exp_b / summed(3)
    dv2 = d * v2
    row_pass(dv2, 4)
    put(ys, 3, dv2 * -SHRINK)
    u3 = exp_a / summed(4)
    col_pass(u3, d, 5)
    put(xs, 0, u3)
    f_out[...] = f1 + jnp.log(u3)
    v3 = exp_b / summed(5)

    y3 = d * v3 * inv_b * cc_ref[...]
    row_pass(y3, 6)
    put(ys, 0, y3 * -SHRINK)
    g_out[...] = g1 + jnp.log(v3)
    x3 = u3 * inv_a * (rc_ref[...] - u3 * summed(6))
    col_pass(x3, d, 7)
    put(xs, 3, x3)
    y2 = dv2 * inv_b * (-v2 * summed(7))
    row_pass(y2, 8)
    put(ys, 1, y2 * -SHRINK)
    x2 = u2 * inv_a * (-u2 * summed(8))
    col_pass(x2, d, 9)
    put(xs, 4, x2)
    y1 = d * inv_b * -summed(9)
    row_pass(y1, 10)
    put(ys, 2, y1 * -SHRINK)

    def thirds(value):
        first = value.astype(BF16).astype(F32)
        rest = value - first
        second = rest.astype(BF16).astype(F32)
        third = (rest - second).astype(BF16).astype(F32)
        return first, second, third

    def stacked(ref, to, order):
        for k in range(NB):
            parts = thirds(ref[k * 8 : (k + 1) * 8, :])
            to[:, k * TB : (k + 1) * TB] = jnp.concatenate(
                [parts[i] for i in order], axis=0
            ).astype(BF16)

    stacked(ys, yb, (0, 1, 0, 2, 0, 1))
    put(xs, 5, inv_a * -summed(10))
    stacked(xs, xb, (0, 0, 1, 0, 2, 1))

    @pl.loop(0, NB // 2)
    def _(k):
        j = lax.rem(col_me // 2 + 1 + k, NB // 2)
        here = block(j, 2 * TB)
        left = nt_dot(unit, xb[:, here]).astype(BF16)
        for cb in range(NB // 2):
            at = slice(cb * 2 * TB, (cb + 1) * 2 * TB)
            factor = jnp.dot(left, yb[:, at], preferred_element_type=F32)
            w[here, at] = (q[here, at] * factor).astype(BF16)
        total = jnp.dot(w[here, :], tgt[...], preferred_element_type=F32)
        for half in range(2):
            peer = j * 2 + half
            gs_send[peer] = total[half * TB : (half + 1) * TB]

            @pl.when(peer != col_me)
            def _():
                pltpu.make_async_remote_copy(
                    src_ref=gs_send.at[peer],
                    dst_ref=gs_land.at[col_me],
                    send_sem=gs_ssem,
                    recv_sem=gs_rsem,
                    device_id={"col": peer},
                    device_id_type=MESH,
                ).start()

    gs_land[col_me] = gs_send[col_me]

    def chip_at(k):
        return lax.rem(z_me + 4 + (1 - 2 * (k % 2)) * ((k + 1) // 2), 8)

    def sibling_copy(j):
        return pltpu.make_async_remote_copy(
            src_ref=gt_part.at[j, 1 - core],
            dst_ref=gt_sib.at[j],
            send_sem=sib_ssem.at[j],
            recv_sem=sib_rsem.at[j],
            device_id={"row": z_me * 2 + 1 - core},
            device_id_type=MESH,
        )

    def pass_on(k):
        j = chip_at(k)
        sibling_copy(j).wait_recv()
        gt_send[j] = gt_part[j, core] + gt_sib[j]

        @pl.when(j != z_me)
        def _():
            pltpu.make_async_remote_copy(
                src_ref=gt_send.at[j],
                dst_ref=gt_land.at[z_me],
                send_sem=gt_ssem,
                recv_sem=gt_rsem,
                device_id={"row": j * 2 + core},
                device_id_type=MESH,
            ).start()

    @pl.loop(0, 8)
    def _(k):
        j = chip_at(k)
        total = jnp.dot(srct[...], w[:, block(j, 2 * TB)], preferred_element_type=F32)
        gt_part[j, 0] = total[:, :TB]
        gt_part[j, 1] = total[:, TB:]
        sibling_copy(j).start()

        @pl.when(k > 0)
        def _():
            pass_on(k - 1)

    pass_on(7)
    gt_land[z_me] = gt_send[z_me]

    others = gs_land.at[pl.ds(0, NB - 1)]
    pltpu.make_async_copy(others, others, gs_rsem).wait()
    for k in range(NB):
        at = slice(k * 8, (k + 1) * 8)
        total = gs_land[0, at, :]
        for i in range(1, NB):
            total += gs_land[i, at, :]
        gs_out[at, :] = total * GROW

    others = gt_land.at[pl.ds(0, 7)]
    pltpu.make_async_copy(others, others, gt_rsem).wait()
    for k in range(NB):
        at = slice(k * 16, (k + 1) * 16)
        total = gt_land[0, at, :]
        for i in range(1, 8):
            total += gt_land[i, at, :]
        gt_out[at, :] = total * GROW

    @pl.loop(0, ROUNDS)
    def _(index):
        others = land.at[index, pl.ds(0, NB - 1)]
        pltpu.make_async_copy(others, others, ar_send.at[index]).wait()

    @pl.loop(0, 8)
    def _(j):
        sibling_copy(j).wait_send()

    others = gs_land.at[pl.ds(0, NB - 1)]
    pltpu.make_async_copy(others, others, gs_ssem).wait()
    others = gt_land.at[pl.ds(0, 7)]
    pltpu.make_async_copy(others, others, gt_ssem).wait()


def on_device(src, tgt, a, b, rows, cols, counts, rc, cc):
    vmem = pl.BlockSpec(memory_space=pltpu.VMEM)
    smem = pl.BlockSpec(memory_space=pltpu.SMEM)
    dma = pltpu.SemaphoreType.DMA
    f, g, gs, gt = pl.pallas_call(
        kernel,
        out_shape=(
            jax.ShapeDtypeStruct((NB, TB), F32),
            jax.ShapeDtypeStruct((NB, TB), F32),
            jax.ShapeDtypeStruct((TB, E), F32),
            jax.ShapeDtypeStruct((E, TB), F32),
        ),
        in_specs=[vmem] * 6 + [smem] + [vmem] * 2,
        out_specs=(vmem,) * 4,
        scratch_shapes=[
            pltpu.VMEM((CELLS, CELLS), F32),
            pltpu.VMEM((CELLS, CELLS), BF16),
            pltpu.VMEM((ROUNDS, NB, TB), F32),
            pltpu.VMEM((ROUNDS, NB, NB, TB), F32),
            pltpu.VMEM((CELLS, TB), F32),
            pltpu.VMEM((CELLS, TB), F32),
            pltpu.VMEM((NB, CELLS), F32),
            pltpu.VMEM((NB, TB), F32),
            pltpu.VMEM((NB, TB), F32),
            pltpu.VMEM((E, CELLS), BF16),
            pltpu.VMEM((NB * 8, TB), F32),
            pltpu.VMEM((NB * 8, TB), F32),
            pltpu.VMEM((48, CELLS), BF16),
            pltpu.VMEM((48, CELLS), BF16),
            pltpu.VMEM((NB, TB, E), F32),
            pltpu.VMEM((NB, TB, E), F32),
            pltpu.VMEM((8, 2, E, TB), F32),
            pltpu.VMEM((8, E, TB), F32),
            pltpu.VMEM((8, E, TB), F32),
            pltpu.VMEM((8, E, TB), F32),
            dma((ROUNDS,)),
            dma((ROUNDS,)),
            dma,
            dma,
            dma((8,)),
            dma((8,)),
            dma,
            dma,
        ],
        compiler_params=pltpu.CompilerParams(
            collective_id=0, has_side_effects=True, vmem_limit_bytes=56 << 20
        ),
    )(
        src,
        tgt,
        a.reshape(NB, TB),
        b.reshape(NB, TB),
        rows.reshape(1, TB),
        cols.reshape(1, TB),
        counts,
        rc.reshape(NB, TB),
        cc.reshape(NB, TB),
    )
    return f.reshape(CELLS), g.reshape(CELLS), gs, gt.T


def solution(mesh):
    placed = (
        P("row", None),
        P("col", None),
        P("row"),
        P("col"),
        P("row", "col", None),
        P("row", "col", None),
        P("row", "col"),
        P("row"),
        P("col"),
    )
    return jax.shard_map(
        on_device,
        mesh=mesh,
        in_specs=placed,
        out_specs=(P("row"), P("col"), P(("row", "col"), None), P(("col", "row"), None)),
        check_vma=False,
    )
```

time: 2040 us -> 133 us (0.07)
  blocking collectives: 1280 us -> 0 us
  waiting for transfers between devices: 375 us -> 0 us
  other arithmetic: 236 us -> 0 us
  Pallas kernels: 0 us -> 128 us
  local copies, waits for them, and re-layouts: 97.6 us -> 3.66 us
    pmax x6 -> x0, blocking collectives: 667 us -> none  [the longest x3 341 us: row_lse(): largest = lax.pmax(partial_max, 'col')]
    psum x11 -> x0, blocking collectives: 610 us -> none  [the longest x3 239 us: on_device(): summed = lax.psum(partial_value, 'col')]
    reduce_scatter x2 -> x0, waiting for transfers between devices: 375 us -> none  [the longest x1 314 us: on_device(): lax.psum_scatter(grad_src, 'col', scatter_dimension=0, tiled=True)]
    pallas_call x0 -> x1, Pallas kernels: none -> 128 us  [on_device(): pl.pallas_call(kernel, out_shape=(jax.ShapeDtypeStruct((NB, TB), F32), ja...]
    gather x136 -> x0, local copies, waits for them, and re-layouts: 85.8 us -> none  [the longest x24 13.3 us: adjoint_advance(): row_blocks[row_ids][:, :, None]]
    dynamic_update_slice x24 -> x0, other arithmetic: 55.7 us -> none  [adjoint_advance(): lax.dynamic_update_slice_in_dim(accum, previous - weighted, first_slot, 0)]
    scatter-add x52 -> x0, other arithmetic: 55 us -> none  [the longest x24 16.3 us: lse_advance(): return (new_max, rescaled.at[own_ids].add(terms))]
    lt x52 -> x0, other arithmetic: 34 us -> none  [fetch(): first_slot + jnp.arange(slots_per_step, dtype=jnp.int32) < live_count]
  transfers between devices with their start and end apart: 2 -> 0, of which waited for: 2 -> 0; matrix products, arithmetic and copies ran while one was open for 0% -> 0% of each run, Pallas kernels for 0% -> 0%
where the time goes in v1:
time: 133 us
  Pallas kernels  128 us (96%)
  local copies, waits for them, and re-layouts  3.66 us (3%)
    pallas_call x1, Pallas kernels, on_device(): pl.pallas_call(kernel, out_shape=(jax.ShapeDtypeStruct((NB, TB), F32), ja...  128 us
    unnamed x10, local copies, waits for them, and re-layouts  3.66 us

profile of v1, /device:TPU:1, one launch (start us, length us, event | category | flops | bytes accessed | tf_op | source)
XLA Modules:
  0.0 132.8 jit_solution(10140859926412027982)
XLA Ops:
  1.3 127.8 %shard_map.120 = (f32[16,128]{1,0:T(8,128)}, f32[16,128]{1,0:T(8,128)}, f32[128,256]{1,0:T(8,128)}, f32[256,128]{1,0:T(8,128)}) custom-call(bf16[2048,256]{1,0:T(8,128)(2,1)} %src.1, bf16[2048,256]{1,0:T(8,128)(2,1)} %tgt.1, f32[16,128]{1,0:T(8,128)} %bitcast.10, f32[16,128]{1,0:T(8,128)} %bitcast.11, s32[1,128]{1,0:T(1,128)} %bitcast.16, ...), custom_call_target="tpu_custom_call" | custom-call | tf_op jit(solution)/shard_map/pallas_call | solution.py:425
  129.1 0.0 copy-start.2
  129.1 0.0 copy-start
  129.1 1.7 %copy.13 = f32[128,256]{1,0:T(8,128)} copy(f32[128,256]{0,1:T(8,128)} %bitcast.9) | data formatting | bytes 262144
  130.8 0.0 copy-done.2
  130.8 0.0 copy-start.1
  130.8 0.6 copy.18
  131.4 0.1 copy-done.1
  131.5 0.6 copy.19
  132.1 0.0 copy-done
  132.1 0.7 copy.20
Async XLA Ops:
  129.1 1.7 %copy-start.2 = (f32[16,128]{1,0:T(8,128)S(1)}, f32[16,128]{1,0:T(8,128)}, u32[]{:S(2)}) copy-start(f32[16,128]{1,0:T(8,128)} %get-tuple-element.8) | copy-start | bytes 24580
  129.1 3.0 %copy-start = (f32[128,256]{1,0:T(8,128)S(1)}, f32[128,256]{1,0:T(8,128)}, u32[]{:S(2)}) copy-start(f32[128,256]{1,0:T(8,128)} %get-tuple-element.22) | copy-start | bytes 393220
  130.8 0.7 copy-start.1

commit v2 on v1

--- a/solution.py
+++ b/solution.py
@@ -11,6 +11,9 @@
 CELLS = NB * TB
 E = 256
 ROUNDS = 11
+HALF = TB // 2
+SUBS = 4
+SUB = E // SUBS
 MASKED = -1e30
 F32 = jnp.float32
 BF16 = jnp.bfloat16
@@ -33,9 +36,9 @@
 def kernel(
     src, tgt, a_ref, b_ref, rows_ref, cols_ref, count_ref, rc_ref, cc_ref,
     f_out, g_out, gs_out, gt_out,
-    q, w, part, land, wide, wide2, bias, vec, vec_w, srct, xs, ys, xb, yb,
-    gs_send, gs_land, gt_part, gt_sib, gt_send, gt_land,
-    ar_send, ar_recv, gs_ssem, gs_rsem, sib_ssem, sib_rsem, gt_ssem, gt_rsem,
+    q, w, w_cols, part, land, wide, wide2, bias, vec, vec_w, srct, xs, ys, xb, yb, xt,
+    gs_sum, gs_last, gs_land, gs_mid, gs_land2, gt_part, gt_sib, gt_sum, gt_land,
+    ar_send, ar_recv, gs_ssem, gs_rsem, gs_ssem2, gs_rsem2, sib_ssem, sib_rsem, gt_ssem, gt_rsem,
 ):
     row_me = lax.axis_index("row")
     col_me = lax.axis_index("col")
@@ -262,6 +265,52 @@
     xs[...] = jnp.zeros_like(xs)
     ys[...] = jnp.zeros_like(ys)
 
+    def thirds(value):
+        first = value.astype(BF16).astype(F32)
+        rest = value - first
+        second = rest.astype(BF16).astype(F32)
+        third = (rest - second).astype(BF16).astype(F32)
+        return first, second, third
+
+    def stacked(ref, to, order):
+        for k in range(NB):
+            parts = thirds(ref[k * 8 : (k + 1) * 8, :])
+            to[:, k * TB : (k + 1) * TB] = jnp.concatenate(
+                [parts[i] for i in order], axis=0
+            ).astype(BF16)
+
+    def stack_x():
+        stacked(xs, xb, (0, 0, 1, 0, 2, 1))
+        for k in range(NB // 2):
+            at = slice(k * 2 * TB, (k + 1) * 2 * TB)
+            xt[at, :] = nt_dot(unit, xb[:, at]).astype(BF16)
+
+    def stack_y():
+        stacked(ys, yb, (0, 1, 0, 2, 0, 1))
+
+    def source_product(into, line, add):
+        if line is not None:
+            vec_w[...] = line
+
+        @pl.loop(0, NB // 4)
+        def _(k):
+            here = block(k, 4 * TB)
+            for cb in range(NB // 2):
+                at = slice(cb * 2 * TB, (cb + 1) * 2 * TB)
+                if line is None:
+                    factor = jnp.dot(xt[here, :], yb[:, at], preferred_element_type=F32)
+                    w[:, at] = (q[here, at] * factor).astype(BF16)
+                else:
+                    for half in range(2):
+                        col = slice((cb * 2 + half) * TB, (cb * 2 + half + 1) * TB)
+                        factor = vec_w[cb * 2 + half : cb * 2 + half + 1, :]
+                        w[:, col] = (q[here, col] * factor).astype(BF16)
+            total = jnp.dot(w[...], tgt[...], preferred_element_type=F32)
+            if add:
+                into[here, :] += total
+            else:
+                into[here, :] = total
+
     row_pass(d, 2)
     put(ys, 4, d * -SHRINK)
     put(ys, 5, jnp.exp(c) * -SHRINK)
@@ -269,6 +318,7 @@
     u2 = exp_a / summed(2)
     col_pass(u2, d, 3)
     put(xs, 1, u2)
+    source_product(gs_last, jnp.exp(c) * -SHRINK, False)
     v2 = exp_b / summed(3)
     dv2 = d * v2
     row_pass(dv2, 4)
@@ -292,54 +342,79 @@
     x2 = u2 * inv_a * (-u2 * summed(8))
     col_pass(x2, d, 9)
     put(xs, 4, x2)
+    stack_x()
+    stack_y()
+    source_product(gs_sum, None, False)
     y1 = d * inv_b * -summed(9)
     row_pass(y1, 10)
     put(ys, 2, y1 * -SHRINK)
-
-    def thirds(value):
-        first = value.astype(BF16).astype(F32)
-        rest = value - first
-        second = rest.astype(BF16).astype(F32)
-        third = (rest - second).astype(BF16).astype(F32)
-        return first, second, third
-
-    def stacked(ref, to, order):
-        for k in range(NB):
-            parts = thirds(ref[k * 8 : (k + 1) * 8, :])
-            to[:, k * TB : (k + 1) * TB] = jnp.concatenate(
-                [parts[i] for i in order], axis=0
-            ).astype(BF16)
-
-    stacked(ys, yb, (0, 1, 0, 2, 0, 1))
-    put(xs, 5, inv_a * -summed(10))
-    stacked(xs, xb, (0, 0, 1, 0, 2, 1))
-
-    @pl.loop(0, NB // 2)
+    stack_y()
+    source_product(gs_sum, y1 * -SHRINK, True)
+    x1 = inv_a * -summed(10)
+    put(xs, 5, x1)
+
+    widen(x1)
+
+    def first_copy(half, other, k):
+        if half == 0:
+            to_x = lax.rem(x_me + k, 4)
+            owner, peer = other * 4 + to_x, y_me * 4 + to_x
+        else:
+            to_y = lax.rem(y_me + k, 4)
+            owner, peer = to_y * 4 + other, to_y * 4 + x_me
+        rows = pl.ds(pl.multiple_of(owner * TB + half * HALF, HALF), HALF)
+        return pltpu.make_async_remote_copy(
+            src_ref=gs_sum.at[rows],
+            dst_ref=gs_land.at[half, other, x_me if half == 0 else y_me],
+            send_sem=gs_ssem.at[half],
+            recv_sem=gs_rsem.at[half, other],
+            device_id={"col": peer},
+            device_id_type=MESH,
+        )
+
+    @pl.loop(0, NB)
+    def _(rb):
+        here = block(rb)
+        u = wide[here, :]
+        for half in range(2):
+            at = slice(half * TB, (half + 1) * TB)
+            gs_sum[here, at] += u * gs_last[here, at]
+
+    def other_at(half, k):
+        return lax.rem((y_me if half == 0 else x_me) + 2 + (1 - 2 * (k % 2)) * ((k + 1) // 2), 4)
+
+    @pl.loop(0, 4)
     def _(k):
-        j = lax.rem(col_me // 2 + 1 + k, NB // 2)
-        here = block(j, 2 * TB)
-        left = nt_dot(unit, xb[:, here]).astype(BF16)
-        for cb in range(NB // 2):
-            at = slice(cb * 2 * TB, (cb + 1) * 2 * TB)
-            factor = jnp.dot(left, yb[:, at], preferred_element_type=F32)
-            w[here, at] = (q[here, at] * factor).astype(BF16)
-        total = jnp.dot(w[here, :], tgt[...], preferred_element_type=F32)
         for half in range(2):
-            peer = j * 2 + half
-            gs_send[peer] = total[half * TB : (half + 1) * TB]
-
-            @pl.when(peer != col_me)
+            for far in (2, 1, 3):
+                first_copy(half, other_at(half, k), far).start()
+
+    def second_stage(k):
+        for half in range(2):
+            other = other_at(half, k)
+            others = gs_land.at[half, other, pl.ds(0, 3)]
+            pltpu.make_async_copy(others, others, gs_rsem.at[half, other]).wait()
+            mine = x_me if half == 0 else y_me
+            owner = other * 4 + x_me if half == 0 else y_me * 4 + other
+            rows = pl.ds(pl.multiple_of(owner * TB + half * HALF, HALF), HALF)
+            total = gs_sum[rows, :]
+            for far in range(1, 4):
+                total += gs_land[half, other, lax.rem(mine + far, 4)]
+            gs_mid[half, other] = total
+
+            @pl.when(k < 3)
             def _():
+                peer = other * 4 + x_me if half == 0 else y_me * 4 + other
                 pltpu.make_async_remote_copy(
-                    src_ref=gs_send.at[peer],
-                    dst_ref=gs_land.at[col_me],
-                    send_sem=gs_ssem,
-                    recv_sem=gs_rsem,
+                    src_ref=gs_mid.at[half, other],
+                    dst_ref=gs_land2.at[half, y_me if half == 0 else x_me],
+                    send_sem=gs_ssem2.at[half],
+                    recv_sem=gs_rsem2.at[half],
                     device_id={"col": peer},
                     device_id_type=MESH,
                 ).start()
 
-    gs_land[col_me] = gs_send[col_me]
+    stack_x()
 
     def chip_at(k):
         return lax.rem(z_me + 4 + (1 - 2 * (k % 2)) * ((k + 1) // 2), 8)
@@ -354,68 +429,106 @@
             device_id_type=MESH,
         )
 
-    def pass_on(k):
+    def ring_copy(way, step, sub):
+        j = lax.rem(z_me + jnp.where(way == 0, 4 - step, 4 + step), 8)
+        rows = pl.ds(sub * SUB, SUB)
+        peer = lax.rem(z_me + jnp.where(way == 0, 1, 7), 8)
+        return pltpu.make_async_remote_copy(
+            src_ref=gt_sum.at[j, rows],
+            dst_ref=gt_land.at[way, step, rows],
+            send_sem=gt_ssem.at[way, step, sub],
+            recv_sem=gt_rsem.at[way, step, sub],
+            device_id={"row": peer * 2 + core},
+            device_id_type=MESH,
+        )
+
+    def ready(k):
         j = chip_at(k)
         sibling_copy(j).wait_recv()
-        gt_send[j] = gt_part[j, core] + gt_sib[j]
-
-        @pl.when(j != z_me)
-        def _():
-            pltpu.make_async_remote_copy(
-                src_ref=gt_send.at[j],
-                dst_ref=gt_land.at[z_me],
-                send_sem=gt_ssem,
-                recv_sem=gt_rsem,
-                device_id={"row": j * 2 + core},
-                device_id_type=MESH,
-            ).start()
+        gt_sum[j] = gt_part[j, core] + gt_sib[j]
+
+    def advance(k):
+        ready(k)
+        j = chip_at(k)
+        way = (k + 1) % 2
+        step = (k + 1) // 2
+        for sub in range(SUBS):
+            rows = pl.ds(sub * SUB, SUB)
+
+            @pl.when((step > 1) | (way == sub // (SUBS // 2)))
+            def _():
+                ring_copy(way, step - 1, sub).wait_recv()
+                gt_sum[j, rows] += gt_land[way, step - 1, rows]
+
+            ring_copy(way, step, sub).start()
 
     @pl.loop(0, 8)
     def _(k):
         j = chip_at(k)
-        total = jnp.dot(srct[...], w[:, block(j, 2 * TB)], preferred_element_type=F32)
+        cols = block(j, 2 * TB)
+        for part_k in range(NB // 4):
+            here = slice(part_k * 4 * TB, (part_k + 1) * 4 * TB)
+            factor = jnp.dot(xt[here, :], yb[:, cols], preferred_element_type=F32)
+            w_cols[here, :] = (q[here, cols] * factor).astype(BF16)
+        total = jnp.dot(srct[...], w_cols[...], preferred_element_type=F32)
         gt_part[j, 0] = total[:, :TB]
         gt_part[j, 1] = total[:, TB:]
         sibling_copy(j).start()
 
-        @pl.when(k > 0)
+        @pl.when(k == 1)
         def _():
-            pass_on(k - 1)
-
-    pass_on(7)
-    gt_land[z_me] = gt_send[z_me]
-
-    others = gs_land.at[pl.ds(0, NB - 1)]
-    pltpu.make_async_copy(others, others, gs_rsem).wait()
-    for k in range(NB):
-        at = slice(k * 8, (k + 1) * 8)
-        total = gs_land[0, at, :]
-        for i in range(1, NB):
-            total += gs_land[i, at, :]
-        gs_out[at, :] = total * GROW
-
-    others = gt_land.at[pl.ds(0, 7)]
-    pltpu.make_async_copy(others, others, gt_rsem).wait()
-    for k in range(NB):
-        at = slice(k * 16, (k + 1) * 16)
-        total = gt_land[0, at, :]
-        for i in range(1, 8):
-            total += gt_land[i, at, :]
-        gt_out[at, :] = total * GROW
+            ready(0)
+            for sub in range(SUBS):
+                ring_copy(sub // (SUBS // 2), 0, sub).start()
+
+        @pl.when(k > 1)
+        def _():
+            advance(k - 1)
+
+        @pl.when(k > 4)
+        def _():
+            second_stage(k - 5)
+
+    ready(7)
+    second_stage(3)
+
+    for way in range(2):
+        for sub in range(SUBS):
+            ring_copy(way, 3, sub).wait_recv()
+    for k in range(2):
+        at = slice(k * TB, (k + 1) * TB)
+        total = gt_sum[z_me, at, :] + gt_land[0, 3, at, :] + gt_land[1, 3, at, :]
+        gt_out[:, at] = (total * GROW).T
+
+    for half in range(2):
+        others = gs_land2.at[half, pl.ds(0, 3)]
+        pltpu.make_async_copy(others, others, gs_rsem2.at[half]).wait()
+        mine = y_me if half == 0 else x_me
+        total = gs_mid[half, mine]
+        for far in range(1, 4):
+            total += gs_land2[half, lax.rem(mine + far, 4)]
+        gs_out[half * HALF : (half + 1) * HALF, :] = total * GROW
 
     @pl.loop(0, ROUNDS)
     def _(index):
         others = land.at[index, pl.ds(0, NB - 1)]
         pltpu.make_async_copy(others, others, ar_send.at[index]).wait()
 
+    for half in range(2):
+        others = gs_land.at[half, pl.ds(0, 3)]
+        pltpu.make_async_copy(others, others, gs_ssem.at[half]).wait()
+        others = gs_land2.at[half, pl.ds(0, 3)]
+        pltpu.make_async_copy(others, others, gs_ssem2.at[half]).wait()
+
     @pl.loop(0, 8)
     def _(j):
         sibling_copy(j).wait_send()
 
-    others = gs_land.at[pl.ds(0, NB - 1)]
-    pltpu.make_async_copy(others, others, gs_ssem).wait()
-    others = gt_land.at[pl.ds(0, 7)]
-    pltpu.make_async_copy(others, others, gt_ssem).wait()
+    for sub in range(SUBS):
+        ring_copy(sub // (SUBS // 2), 0, sub).wait_send()
+        for way in range(2):
+            for step in range(1, 4):
+                ring_copy(way, step, sub).wait_send()
 
 
 def on_device(src, tgt, a, b, rows, cols, counts, rc, cc):
@@ -428,13 +541,14 @@
             jax.ShapeDtypeStruct((NB, TB), F32),
             jax.ShapeDtypeStruct((NB, TB), F32),
             jax.ShapeDtypeStruct((TB, E), F32),
-            jax.ShapeDtypeStruct((E, TB), F32),
+            jax.ShapeDtypeStruct((TB, E), F32),
         ),
         in_specs=[vmem] * 6 + [smem] + [vmem] * 2,
         out_specs=(vmem,) * 4,
         scratch_shapes=[
             pltpu.VMEM((CELLS, CELLS), F32),
-            pltpu.VMEM((CELLS, CELLS), BF16),
+            pltpu.VMEM((4 * TB, CELLS), BF16),
+            pltpu.VMEM((CELLS, 2 * TB), BF16),
             pltpu.VMEM((ROUNDS, NB, TB), F32),
             pltpu.VMEM((ROUNDS, NB, NB, TB), F32),
             pltpu.VMEM((CELLS, TB), F32),
@@ -447,20 +561,26 @@
             pltpu.VMEM((NB * 8, TB), F32),
             pltpu.VMEM((48, CELLS), BF16),
             pltpu.VMEM((48, CELLS), BF16),
-            pltpu.VMEM((NB, TB, E), F32),
-            pltpu.VMEM((NB, TB, E), F32),
+            pltpu.VMEM((CELLS, 48), BF16),
+            pltpu.VMEM((CELLS, E), F32),
+            pltpu.VMEM((CELLS, E), F32),
+            pltpu.VMEM((2, 4, 4, HALF, E), F32),
+            pltpu.VMEM((2, 4, HALF, E), F32),
+            pltpu.VMEM((2, 4, HALF, E), F32),
             pltpu.VMEM((8, 2, E, TB), F32),
             pltpu.VMEM((8, E, TB), F32),
             pltpu.VMEM((8, E, TB), F32),
-            pltpu.VMEM((8, E, TB), F32),
+            pltpu.VMEM((2, 4, E, TB), F32),
             dma((ROUNDS,)),
             dma((ROUNDS,)),
-            dma,
-            dma,
+            dma((2,)),
+            dma((2, 4)),
+            dma((2,)),
+            dma((2,)),
             dma((8,)),
             dma((8,)),
-            dma,
-            dma,
+            dma((2, 4, SUBS)),
+            dma((2, 4, SUBS)),
         ],
         compiler_params=pltpu.CompilerParams(
             collective_id=0, has_side_effects=True, vmem_limit_bytes=56 << 20
@@ -476,7 +596,7 @@
         rc.reshape(NB, TB),
         cc.reshape(NB, TB),
     )
-    return f.reshape(CELLS), g.reshape(CELLS), gs, gt.T
+    return f.reshape(CELLS), g.reshape(CELLS), gs, gt
 
 
 def solution(mesh):

time: 133 us -> 120 us (0.902)
  Pallas kernels: 128 us -> 114 us
    pallas_call x1, Pallas kernels: 128 us -> 114 us  [on_device(): pl.pallas_call(kernel, out_shape=(jax.ShapeDtypeStruct((NB, TB), F32), ja...]
where the time goes in v2:
time: 120 us
  Pallas kernels  114 us (95%)
  local copies, waits for them, and re-layouts  4.25 us (4%)
  between operations  1.3 us (1%)
    pallas_call x1, Pallas kernels, on_device(): pl.pallas_call(kernel, out_shape=(jax.ShapeDtypeStruct((NB, TB), F32), ja...  114 us
    unnamed x10, local copies, waits for them, and re-layouts  4.25 us

profile of v2, /device:TPU:1, one launch (start us, length us, event | category | flops | bytes accessed | tf_op | source)
XLA Modules:
  0.0 119.6 jit_solution(7256300213846978890)
XLA Ops:
  1.3 114.1 %shard_map.120 = (f32[16,128]{1,0:T(8,128)}, f32[16,128]{1,0:T(8,128)}, f32[128,256]{1,0:T(8,128)}, f32[128,256]{1,0:T(8,128)}) custom-call(bf16[2048,256]{1,0:T(8,128)(2,1)} %src.1, bf16[2048,256]{1,0:T(8,128)(2,1)} %tgt.1, f32[16,128]{1,0:T(8,128)} %bitcast.8, f32[16,128]{1,0:T(8,128)} %bitcast.9, s32[1,128]{1,0:T(1,128)} %bitcast.14, s32[1,128]{1,0:T(1,128)} %bitcast.15, ...), custom_call_target="tpu_custom_call" | custom-call | tf_op jit(solution)/shard_map/pallas_call | solution.py:538
  115.4 0.0 copy-start.2
  115.4 0.7 copy-done.2
  116.1 0.0 copy-start.1
  116.1 0.6 copy.18
  116.7 0.1 copy-done.1
  116.8 0.6 copy.19
  117.4 0.0 copy-start
  117.4 1.6 %copy.20 = f32[128,256]{1,0:T(8,128)} copy(f32[128,256]{1,0:T(8,128)} %get-tuple-element.18) | data formatting | bytes 262144
  119.0 0.0 copy-done
  119.0 0.7 copy.21
Async XLA Ops:
  115.4 0.7 copy-start.2
  116.1 0.7 copy-start.1
  117.4 1.6 %copy-start = (f32[128,256]{1,0:T(8,128)S(1)}, f32[128,256]{1,0:T(8,128)}, u32[]{:S(2)}) copy-start(f32[128,256]{1,0:T(8,128)} %get-tuple-element.19) | copy-start | bytes 393220

commit v3 on v2

--- a/solution.py
+++ b/solution.py
@@ -11,8 +11,9 @@
 CELLS = NB * TB
 E = 256
 ROUNDS = 11
+TALL = 8
 HALF = TB // 2
-SUBS = 4
+SUBS = 2
 SUB = E // SUBS
 MASKED = -1e30
 F32 = jnp.float32
@@ -36,7 +37,7 @@
 def kernel(
     src, tgt, a_ref, b_ref, rows_ref, cols_ref, count_ref, rc_ref, cc_ref,
     f_out, g_out, gs_out, gt_out,
-    q, w, w_cols, part, land, wide, wide2, bias, vec, vec_w, srct, xs, ys, xb, yb, xt,
+    q, most, w, w_cols, part, land, wide, wide2, bias, vec, vec_w, srct, xs, ys, xb, yb, xt,
     gs_sum, gs_last, gs_land, gs_mid, gs_land2, gt_part, gt_sib, gt_sum, gt_land,
     ar_send, ar_recv, gs_ssem, gs_rsem, gs_ssem2, gs_rsem2, sib_ssem, sib_rsem, gt_ssem, gt_rsem,
 ):
@@ -77,7 +78,7 @@
 
     slot = lax.broadcasted_iota(jnp.int32, (TB, TB), 1)
     which = lax.broadcasted_iota(jnp.int32, (TB, TB), 0)
-    live = slot < count_ref[0, 0]
+    live = slot < count_ref[...]
     row_hot = jnp.where((rows_ref[...] == which) & live, 1.0, 0.0).astype(BF16)
     col_hot = jnp.where((cols_ref[...] == which) & live, 1.0, 0.0).astype(BF16)
     present = nt_dot(row_hot[:NB], col_hot).astype(BF16)
@@ -86,26 +87,27 @@
         hits = jnp.dot(present, spread, preferred_element_type=F32)
         bias[:, cb * TB : (cb + 1) * TB] = jnp.where(hits > 0.5, 0.0, MASKED)
 
-    @pl.loop(0, NB // 2)
-    def _(rb):
-        top = None
-        left = src[block(rb, 2 * TB), :]
+    @pl.loop(0, NB // TALL)
+    def _(k):
+        left = src[block(k, TALL * TB), :]
         for cb in range(NB // 2):
             at = slice(cb * 2 * TB, (cb + 1) * 2 * TB)
             s = nt_dot(left, tgt[at, :])
-            for half in range(2):
-                line = bias[pl.ds(rb * 2 + half, 1), at]
-                q[block(rb * 2 + half), at] = s[half * TB : (half + 1) * TB] + line
-        for half in range(2):
-            here = block(rb * 2 + half)
-            top = q[here, 0:TB]
-            for cb in range(1, NB):
-                top = jnp.maximum(top, q[here, cb * TB : (cb + 1) * TB])
-            total = jnp.exp(q[here, 0:TB] - top)
-            for cb in range(1, NB):
-                total += jnp.exp(q[here, cb * TB : (cb + 1) * TB] - top)
-            wide[here, :] = top
-            wide2[here, :] = total
+            for i in range(TALL):
+                line = bias[pl.ds(k * TALL + i, 1), at]
+                q[block(k * TALL + i), at] = s[i * TB : (i + 1) * TB] + line
+
+    @pl.loop(0, NB)
+    def _(rb):
+        here = block(rb)
+        top = q[here, 0:TB]
+        for cb in range(1, NB):
+            top = jnp.maximum(top, q[here, cb * TB : (cb + 1) * TB])
+        total = jnp.exp(q[here, 0:TB] - top)
+        for cb in range(1, NB):
+            total += jnp.exp(q[here, cb * TB : (cb + 1) * TB] - top)
+        wide[here, :] = top
+        wide2[here, :] = total
 
     for rb in range(NB):
         here = slice(rb * TB, (rb + 1) * TB)
@@ -119,8 +121,7 @@
     def start_reduce(index, axis):
         me = row_me if axis == "row" else col_me
 
-        @pl.loop(0, NB - 1)
-        def _(k):
+        def send(k, carry):
             if axis == "row":
                 j = k // 2
                 far = lax.rem(4 + (1 - 2 * (j % 2)) * ((j + 1) // 2), 8)
@@ -139,7 +140,9 @@
                 device_id={axis: peer},
                 device_id_type=MESH,
             ).start()
-
+            return carry
+
+        lax.fori_loop(0, NB - 1, send, 0, unroll=True)
         land[index, me] = part[index]
 
     def end_reduce(index):
@@ -288,37 +291,27 @@
     def stack_y():
         stacked(ys, yb, (0, 1, 0, 2, 0, 1))
 
-    def source_product(into, line, add):
-        if line is not None:
-            vec_w[...] = line
-
-        @pl.loop(0, NB // 4)
+    def source_product(into, line, with_most):
+        vec_w[...] = line
+
+        @pl.loop(0, NB // TALL)
         def _(k):
-            here = block(k, 4 * TB)
-            for cb in range(NB // 2):
-                at = slice(cb * 2 * TB, (cb + 1) * 2 * TB)
-                if line is None:
-                    factor = jnp.dot(xt[here, :], yb[:, at], preferred_element_type=F32)
-                    w[:, at] = (q[here, at] * factor).astype(BF16)
-                else:
-                    for half in range(2):
-                        col = slice((cb * 2 + half) * TB, (cb * 2 + half + 1) * TB)
-                        factor = vec_w[cb * 2 + half : cb * 2 + half + 1, :]
-                        w[:, col] = (q[here, col] * factor).astype(BF16)
-            total = jnp.dot(w[...], tgt[...], preferred_element_type=F32)
-            if add:
-                into[here, :] += total
-            else:
-                into[here, :] = total
-
+            here = block(k, TALL * TB)
+            for cb in range(NB):
+                col = slice(cb * TB, (cb + 1) * TB)
+                value = q[here, col] * vec_w[cb : cb + 1, :]
+                if with_most:
+                    value += most[here, col]
+                w[:, col] = value.astype(BF16)
+            into[here, :] = jnp.dot(w[...], tgt[...], preferred_element_type=F32)
+
+    last_line = jnp.exp(c) * -SHRINK
     row_pass(d, 2)
     put(ys, 4, d * -SHRINK)
-    put(ys, 5, jnp.exp(c) * -SHRINK)
-    put(xs, 2, jnp.ones_like(a))
     u2 = exp_a / summed(2)
     col_pass(u2, d, 3)
     put(xs, 1, u2)
-    source_product(gs_last, jnp.exp(c) * -SHRINK, False)
+    source_product(gs_last, last_line, False)
     v2 = exp_b / summed(3)
     dv2 = d * v2
     row_pass(dv2, 4)
@@ -344,14 +337,19 @@
     put(xs, 4, x2)
     stack_x()
     stack_y()
-    source_product(gs_sum, None, False)
+
+    @pl.loop(0, NB // TALL)
+    def _(k):
+        here = block(k, TALL * TB)
+        for cb in range(NB // 2):
+            at = slice(cb * 2 * TB, (cb + 1) * 2 * TB)
+            factor = jnp.dot(xt[here, :], yb[:, at], preferred_element_type=F32)
+            most[here, at] = q[here, at] * factor
+
     y1 = d * inv_b * -summed(9)
     row_pass(y1, 10)
-    put(ys, 2, y1 * -SHRINK)
-    stack_y()
     source_product(gs_sum, y1 * -SHRINK, True)
     x1 = inv_a * -summed(10)
-    put(xs, 5, x1)
 
     widen(x1)
 
@@ -372,22 +370,8 @@
             device_id_type=MESH,
         )
 
-    @pl.loop(0, NB)
-    def _(rb):
-        here = block(rb)
-        u = wide[here, :]
-        for half in range(2):
-            at = slice(half * TB, (half + 1) * TB)
-            gs_sum[here, at] += u * gs_last[here, at]
-
     def other_at(half, k):
         return lax.rem((y_me if half == 0 else x_me) + 2 + (1 - 2 * (k % 2)) * ((k + 1) // 2), 4)
-
-    @pl.loop(0, 4)
-    def _(k):
-        for half in range(2):
-            for far in (2, 1, 3):
-                first_copy(half, other_at(half, k), far).start()
 
     def second_stage(k):
         for half in range(2):
@@ -414,7 +398,23 @@
                     device_id_type=MESH,
                 ).start()
 
-    stack_x()
+    def first_stage():
+        @pl.loop(0, NB)
+        def _(rb):
+            here = block(rb)
+            u = wide[here, :]
+            for half in range(2):
+                at = slice(half * TB, (half + 1) * TB)
+                gs_sum[here, at] += u * gs_last[here, at]
+
+        @pl.loop(0, 4)
+        def _(k):
+            for half in range(2):
+                for far in (2, 1, 3):
+                    first_copy(half, other_at(half, k), far).start()
+
+    vec_w[...] = last_line
+    vec[...] = y1 * -SHRINK
 
     def chip_at(k):
         return lax.rem(z_me + 4 + (1 - 2 * (k % 2)) * ((k + 1) // 2), 8)
@@ -466,14 +466,23 @@
     def _(k):
         j = chip_at(k)
         cols = block(j, 2 * TB)
-        for part_k in range(NB // 4):
-            here = slice(part_k * 4 * TB, (part_k + 1) * 4 * TB)
-            factor = jnp.dot(xt[here, :], yb[:, cols], preferred_element_type=F32)
-            w_cols[here, :] = (q[here, cols] * factor).astype(BF16)
+        for part_k in range(NB // 2):
+            here = slice(part_k * 2 * TB, (part_k + 1) * 2 * TB)
+            u = wide[here, :]
+            for half in range(2):
+                col = block(j * 2 + half)
+                last = vec_w[pl.ds(j * 2 + half, 1), :]
+                line = vec[pl.ds(j * 2 + half, 1), :]
+                value = most[here, col] + q[here, col] * (line + u * last)
+                w_cols[here, half * TB : (half + 1) * TB] = value.astype(BF16)
         total = jnp.dot(srct[...], w_cols[...], preferred_element_type=F32)
         gt_part[j, 0] = total[:, :TB]
         gt_part[j, 1] = total[:, TB:]
         sibling_copy(j).start()
+
+        @pl.when(k == 0)
+        def _():
+            first_stage()
 
         @pl.when(k == 1)
         def _():
@@ -533,7 +542,6 @@
 
 def on_device(src, tgt, a, b, rows, cols, counts, rc, cc):
     vmem = pl.BlockSpec(memory_space=pltpu.VMEM)
-    smem = pl.BlockSpec(memory_space=pltpu.SMEM)
     dma = pltpu.SemaphoreType.DMA
     f, g, gs, gt = pl.pallas_call(
         kernel,
@@ -543,11 +551,12 @@
             jax.ShapeDtypeStruct((TB, E), F32),
             jax.ShapeDtypeStruct((TB, E), F32),
         ),
-        in_specs=[vmem] * 6 + [smem] + [vmem] * 2,
+        in_specs=[vmem] * 9,
         out_specs=(vmem,) * 4,
         scratch_shapes=[
             pltpu.VMEM((CELLS, CELLS), F32),
-            pltpu.VMEM((4 * TB, CELLS), BF16),
+            pltpu.VMEM((CELLS, CELLS), F32),
+            pltpu.VMEM((TALL * TB, CELLS), BF16),
             pltpu.VMEM((CELLS, 2 * TB), BF16),
             pltpu.VMEM((ROUNDS, NB, TB), F32),
             pltpu.VMEM((ROUNDS, NB, NB, TB), F32),
@@ -583,7 +592,7 @@
             dma((2, 4, SUBS)),
         ],
         compiler_params=pltpu.CompilerParams(
-            collective_id=0, has_side_effects=True, vmem_limit_bytes=56 << 20
+            collective_id=0, has_side_effects=True, vmem_limit_bytes=60 << 20
         ),
     )(
         src,

time: 120 us -> 116 us (0.967)
  Pallas kernels: 114 us -> 110 us
    pallas_call x1, Pallas kernels: 114 us -> 110 us  [on_device(): pl.pallas_call(kernel, out_shape=(jax.ShapeDtypeStruct((NB, TB), F32), ja...]
where the time goes in v3:
time: 116 us
  Pallas kernels  110 us (95%)
  local copies, waits for them, and re-layouts  4.25 us (4%)
  between operations  1.3 us (1%)
    pallas_call x1, Pallas kernels, on_device(): pl.pallas_call(kernel, out_shape=(jax.ShapeDtypeStruct((NB, TB), F32), ja...  110 us
    unnamed x10, local copies, waits for them, and re-layouts  4.25 us

profile of v3, /device:TPU:1, one launch (start us, length us, event | category | flops | bytes accessed | tf_op | source)
XLA Modules:
  0.0 115.6 jit_solution(10730754664613559431)
XLA Ops:
  1.3 110.1 %shard_map.120 = (f32[16,128]{1,0:T(8,128)}, f32[16,128]{1,0:T(8,128)}, f32[128,256]{1,0:T(8,128)}, f32[128,256]{1,0:T(8,128)}) custom-call(bf16[2048,256]{1,0:T(8,128)(2,1)} %src.1, bf16[2048,256]{1,0:T(8,128)(2,1)} %tgt.1, f32[16,128]{1,0:T(8,128)} %bitcast.8, f32[16,128]{1,0:T(8,128)} %bitcast.9, s32[1,128]{1,0:T(1,128)} %bitcast.14, s32[1,128]{1,0:T(1,128)} %bitcast.15, ...), custom_call_target="tpu_custom_call" | custom-call | tf_op jit(solution)/shard_map/pallas_call | solution.py:546
  111.4 0.0 copy-start.2
  111.4 0.7 copy-done.2
  112.1 0.0 copy-start.1
  112.1 0.6 copy.18
  112.7 0.1 copy-done.1
  112.8 0.6 copy.19
  113.4 0.0 copy-start
  113.4 1.6 %copy.20 = f32[128,256]{1,0:T(8,128)} copy(f32[128,256]{1,0:T(8,128)} %get-tuple-element.18) | data formatting | bytes 262144
  115.0 0.0 copy-done
  115.0 0.7 copy.21
Async XLA Ops:
  111.4 0.7 copy-start.2
  112.1 0.7 copy-start.1
  113.4 1.6 %copy-start = (f32[128,256]{1,0:T(8,128)S(1)}, f32[128,256]{1,0:T(8,128)}, u32[]{:S(2)}) copy-start(f32[128,256]{1,0:T(8,128)} %get-tuple-element.19) | copy-start | bytes 393220

commit v4 on v3

--- a/solution.py
+++ b/solution.py
@@ -319,13 +319,13 @@
     u3 = exp_a / summed(4)
     col_pass(u3, d, 5)
     put(xs, 0, u3)
-    f_out[...] = f1 + jnp.log(u3)
+    f_out[...] = -(f1 + jnp.log(u3))
     v3 = exp_b / summed(5)
 
     y3 = d * v3 * inv_b * cc_ref[...]
     row_pass(y3, 6)
     put(ys, 0, y3 * -SHRINK)
-    g_out[...] = g1 + jnp.log(v3)
+    g_out[...] = -(g1 + jnp.log(v3))
     x3 = u3 * inv_a * (rc_ref[...] - u3 * summed(6))
     col_pass(x3, d, 7)
     put(xs, 3, x3)
@@ -507,7 +507,7 @@
     for k in range(2):
         at = slice(k * TB, (k + 1) * TB)
         total = gt_sum[z_me, at, :] + gt_land[0, 3, at, :] + gt_land[1, 3, at, :]
-        gt_out[:, at] = (total * GROW).T
+        gt_out[:, at] = total.T
 
     for half in range(2):
         others = gs_land2.at[half, pl.ds(0, 3)]
@@ -516,7 +516,7 @@
         total = gs_mid[half, mine]
         for far in range(1, 4):
             total += gs_land2[half, lax.rem(mine + far, 4)]
-        gs_out[half * HALF : (half + 1) * HALF, :] = total * GROW
+        gs_out[half * HALF : (half + 1) * HALF, :] = total
 
     @pl.loop(0, ROUNDS)
     def _(index):
@@ -605,7 +605,7 @@
         rc.reshape(NB, TB),
         cc.reshape(NB, TB),
     )
-    return f.reshape(CELLS), g.reshape(CELLS), gs, gt
+    return -f.reshape(CELLS), -g.reshape(CELLS), gs * GROW, gt * GROW
 
 
 def solution(mesh):

time: 116 us -> 115 us (level)
  local copies, waits for them, and re-layouts: 4.25 us -> 0 us
  other arithmetic: 0 us -> 3.01 us
    unnamed x10 -> x0, local copies, waits for them, and re-layouts: 4.25 us -> none
    mul x0 -> x1, other arithmetic: none -> 1.68 us  [on_device(): return (-f.reshape(CELLS), -g.reshape(CELLS), gs * GROW, gt * GROW)]
    neg x0 -> x1, other arithmetic: none -> 1.32 us  [on_device(): return (-f.reshape(CELLS), -g.reshape(CELLS), gs * GROW, gt * GROW)]
where the time goes in v4:
time: 115 us; the launch traced here: 114 us
  Pallas kernels  110 us (96%)
  other arithmetic  3.01 us (3%)
  between operations  1.29 us (1%)
    pallas_call x1, Pallas kernels, on_device(): pl.pallas_call(kernel, out_shape=(jax.ShapeDtypeStruct((NB, TB), F32), ja...  110 us

profile of v4, /device:TPU:1, one launch (start us, length us, event | category | flops | bytes accessed | tf_op | source)
XLA Modules:
  0.0 114.4 jit_solution(12891094047668280821)
XLA Ops:
  1.3 110.1 %shard_map.120 = (f32[16,128]{1,0:T(8,128)}, f32[16,128]{1,0:T(8,128)}, f32[128,256]{1,0:T(8,128)}, f32[128,256]{1,0:T(8,128)}) custom-call(bf16[2048,256]{1,0:T(8,128)(2,1)} %src.1, bf16[2048,256]{1,0:T(8,128)(2,1)} %tgt.1, f32[16,128]{1,0:T(8,128)} %bitcast.10, f32[16,128]{1,0:T(8,128)} %bitcast.11, s32[1,128]{1,0:T(1,128)} %bitcast.14, ...), custom_call_target="tpu_custom_call" | custom-call | tf_op jit(solution)/shard_map/pallas_call | solution.py:546
  111.4 1.3 %negate_bitcast_fusion = (f32[2048]{0:T(1024)}, f32[2048]{0:T(1024)}) fusion(f32[16,128]{1,0:T(8,128)} %get-tuple-element.9, f32[16,128]{1,0:T(8,128)} %get-tuple-element.8), kind=kLoop, calls=%fused_computation.2 | loop fusion | flops 4096 | bytes 32768 | tf_op jit(solution)/shard_map/neg | solution.py:608
  112.7 1.7 %broadcast_multiply_fusion = (f32[128,256]{1,0:T(8,128)}, f32[128,256]{1,0:T(8,128)}) fusion(f32[128,256]{1,0:T(8,128)} %get-tuple-element.11, f32[128,256]{1,0:T(8,128)} %get-tuple-element.10), kind=kLoop, calls=%fused_computation | loop fusion | flops 65536 | bytes 524288 | tf_op jit(solution)/shard_map/mul | solution.py:608

commit v5 on v4

--- a/solution.py
+++ b/solution.py
@@ -431,7 +431,7 @@
 
     def ring_copy(way, step, sub):
         j = lax.rem(z_me + jnp.where(way == 0, 4 - step, 4 + step), 8)
-        rows = pl.ds(sub * SUB, SUB)
+        rows = pl.ds(pl.multiple_of(sub * SUB, SUB), SUB)
         peer = lax.rem(z_me + jnp.where(way == 0, 1, 7), 8)
         return pltpu.make_async_remote_copy(
             src_ref=gt_sum.at[j, rows],
@@ -452,10 +452,11 @@
         j = chip_at(k)
         way = (k + 1) % 2
         step = (k + 1) // 2
-        for sub in range(SUBS):
-            rows = pl.ds(sub * SUB, SUB)
-
-            @pl.when((step > 1) | (way == sub // (SUBS // 2)))
+        for i in range(SUBS):
+            sub = (1 - way) * (1 - i) + way * i
+            rows = pl.ds(pl.multiple_of(sub * SUB, SUB), SUB)
+
+            @pl.when((step > 1) | (way == sub))
             def _():
                 ring_copy(way, step - 1, sub).wait_recv()
                 gt_sum[j, rows] += gt_land[way, step - 1, rows]

time: 115 us -> 116 us (level)
  no operation moved by 1% of the time
where the time goes in v5:
time: 116 us; the launch traced here: 115 us
  Pallas kernels  111 us (96%)
  other arithmetic  3.01 us (3%)
  between operations  1.29 us (1%)
    pallas_call x1, Pallas kernels, on_device(): pl.pallas_call(kernel, out_shape=(jax.ShapeDtypeStruct((NB, TB), F32), ja...  111 us

profile of v5, /device:TPU:1, one launch (start us, length us, event | category | flops | bytes accessed | tf_op | source)
XLA Modules:
  0.0 115.3 jit_solution(7298821721272829494)
XLA Ops:
  1.3 111.0 %shard_map.120 = (f32[16,128]{1,0:T(8,128)}, f32[16,128]{1,0:T(8,128)}, f32[128,256]{1,0:T(8,128)}, f32[128,256]{1,0:T(8,128)}) custom-call(bf16[2048,256]{1,0:T(8,128)(2,1)} %src.1, bf16[2048,256]{1,0:T(8,128)(2,1)} %tgt.1, f32[16,128]{1,0:T(8,128)} %bitcast.10, f32[16,128]{1,0:T(8,128)} %bitcast.11, s32[1,128]{1,0:T(1,128)} %bitcast.14, ...), custom_call_target="tpu_custom_call" | custom-call | tf_op jit(solution)/shard_map/pallas_call | solution.py:547
  112.3 1.3 %negate_bitcast_fusion = (f32[2048]{0:T(1024)}, f32[2048]{0:T(1024)}) fusion(f32[16,128]{1,0:T(8,128)} %get-tuple-element.9, f32[16,128]{1,0:T(8,128)} %get-tuple-element.8), kind=kLoop, calls=%fused_computation.2 | loop fusion | flops 4096 | bytes 32768 | tf_op jit(solution)/shard_map/neg | solution.py:609
  113.6 1.7 %broadcast_multiply_fusion = (f32[128,256]{1,0:T(8,128)}, f32[128,256]{1,0:T(8,128)}) fusion(f32[128,256]{1,0:T(8,128)} %get-tuple-element.11, f32[128,256]{1,0:T(8,128)} %get-tuple-element.10), kind=kLoop, calls=%fused_computation | loop fusion | flops 65536 | bytes 524288 | tf_op jit(solution)/shard_map/mul | solution.py:609
